TPU v7x, 256 devices: a whole 4x4x8 slice. The times are simulated.
256 devices in a mesh: layer: 4 (over y_hi, core), rows: 4 (over x), feat: 16 (over z, y_lo).
Axes of the slice: x: 4, y: 4 (y_hi: 2, y_lo: 2; y = y_hi * 2 + y_lo), z: 8, core: 2. Of those that a mesh axis runs over, the one named last changes fastest.
Arguments:
- resid: bfloat16 [4, 512, 2304], P('layer', 'rows'), may hold values from -6 to 6
- norm_gain: float32 [4, 2304], P('layer'), may hold values from 0.5 to 2
- gate_weight: bfloat16 [4, 9216, 2304], P('layer', ('rows', 'feat')), may hold values from -0.125 to 0.125
- up_weight: bfloat16 [4, 9216, 2304], P('layer', ('rows', 'feat')), may hold values from -0.125 to 0.125
- down_weight: bfloat16 [4, 9216, 2304], P('layer', ('rows', 'feat')), may hold values from -0.0625 to 0.0625
- enc_weight: bfloat16 [4, 2304, 32768], P('layer', None, ('rows', 'feat')), may hold values from -0.125 to 0.125
- enc_bias: float32 [4, 32768], P('layer', ('rows', 'feat')), may hold values from -3 to 3
- dec_weight: bfloat16 [10, 32768, 2304], P(None, ('rows', 'feat'), 'layer'), may hold values from -0.03125 to 0.03125
- dec_bias: float32 [4, 2304], P(None, 'layer'), may hold values from -3 to 3
Outputs:
- errors: bfloat16 [512, 4, 2304], P(('rows', 'feat'), None, 'layer')
- act_grad: bfloat16 [4, 512, 32768], P('layer', None, ('rows', 'feat'))
All inputs are finite; a program needn't handle non-finite values.
Results may differ from a plain program's by a relative error of at most 0.017.
Values may be sent and summed in bfloat16 or wider, within the bound.
A program may use at most 128 MiB of HBM per device.

v0:
```python
import jax
import jax.numpy as jnp
from jax import lax
from jax.sharding import PartitionSpec as P


def pair_index(source, target, layers):
    return source * layers - source * (source - 1) // 2 + target - source


def normalize(resid_rows, gain_row):
    as_float = resid_rows.astype(jnp.float32)
    inv_rms = lax.rsqrt(jnp.mean(as_float * as_float, axis=-1, keepdims=True) + 1e-06)
    return (as_float * inv_rms * gain_row).astype(jnp.bfloat16)


def contract_last(left, right):
    return lax.dot_general(
        left, right, (((1,), (1,)), ((), ())), preferred_element_type=jnp.float32
    )


def decode_rows(features_all, dec_weight, target, layers, row_count):
    running = jnp.zeros((row_count, dec_weight.shape[2]), jnp.float32)
    for source in range(target + 1):
        row_block = features_all[source]
        running = running + jnp.dot(
            row_block,
            dec_weight[pair_index(source, target, layers)],
            preferred_element_type=jnp.float32,
        )
    return running


def body(
    resid,
    norm_gain,
    gate_weight,
    up_weight,
    down_weight,
    enc_weight,
    enc_bias,
    dec_weight,
    dec_bias,
):
    layers = lax.axis_size("layer")
    keep_rows = (
        resid.shape[1] * lax.axis_size("rows") // (lax.axis_size("rows") * lax.axis_size("feat"))
    )
    normed = normalize(resid[0], norm_gain[0])
    whole = lax.all_gather(normed, "rows", axis=0, tiled=True)
    gate_proj = contract_last(whole, gate_weight[0])
    up_proj = contract_last(whole, up_weight[0])
    hidden = (jax.nn.gelu(gate_proj, approximate=True) * up_proj).astype(jnp.bfloat16)
    mlp_part = jnp.dot(hidden, down_weight[0], preferred_element_type=jnp.float32)
    pre_act = jnp.dot(whole, enc_weight[0], preferred_element_type=jnp.float32) + enc_bias[0]
    features = jnp.maximum(pre_act, 0.0).astype(jnp.bfloat16)
    features_all = lax.all_gather(features[None], "layer", axis=0, tiled=True)
    mlp_rows = None
    reduced = lax.psum_scatter(mlp_part, ("rows", "feat"), scatter_dimension=0, tiled=True)
    mlp_rows = lax.all_to_all(
        reduced[:, None, :].astype(jnp.bfloat16), "layer", split_axis=2, concat_axis=1, tiled=True
    ).astype(jnp.float32)

    def target_term(target, row_count):
        partial_value = decode_rows(features_all, dec_weight, target, layers, row_count)
        return partial_value

    pieces = []
    for target in range(layers):

        def term_one(first_row, row_count, target=target):
            return target_term(target, row_count)

        pieces.append(
            lax.psum_scatter(
                term_one(jnp.int32(0), lax.axis_size(("rows", "feat")) * keep_rows),
                ("rows", "feat"),
                scatter_dimension=0,
                tiled=True,
            )
        )
    summed = jnp.stack(pieces, 1)
    error_f32 = summed + dec_bias[None]
    error_f32 = error_f32 - mlp_rows
    errors = error_f32.astype(jnp.bfloat16)
    shard_rows = lax.all_gather(errors, ("rows", "feat"), axis=0, tiled=True)
    per_source = []
    for source in range(layers):
        running = jnp.zeros((shard_rows.shape[0], dec_weight.shape[1]), jnp.float32)
        for target in range(source, layers):
            running = running + contract_last(
                shard_rows[:, target, :], dec_weight[pair_index(source, target, layers)]
            )
        per_source.append(running)
    gradients = jnp.stack(per_source, 0)
    act_grad = lax.psum_scatter(
        gradients.astype(jnp.bfloat16), "layer", scatter_dimension=0, tiled=True
    )
    return (errors, act_grad)


def solution(mesh):
    in_specs = (
        P("layer", "rows", None),
        P("layer", None),
        P("layer", ("rows", "feat"), None),
        P("layer", ("rows", "feat"), None),
        P("layer", ("rows", "feat"), None),
        P("layer", None, ("rows", "feat")),
        P("layer", ("rows", "feat")),
        P(None, ("rows", "feat"), "layer"),
        P(None, "layer"),
    )
    out_specs = (P(("rows", "feat"), None, "layer"), P("layer", None, ("rows", "feat")))
    return jax.shard_map(body, mesh=mesh, in_specs=in_specs, out_specs=out_specs, check_vma=False)
```

profile of v0, /device:TPU:6, one launch (start us, length us, event | category | flops | bytes accessed | tf_op | source)
XLA Modules:
  0.0 1470.9 jit_solution(9936259430973415305)
XLA Ops:
  9.4 2.1 fusion.20
  11.6 36.7 %all-gather.5.cloned.1.call-done = bf16[512,2304]{1,0:T(8,128)(2,1)} async-done(((bf16[128,2304]{1,0:T(8,128)(2,1)}), bf16[512,2304]{1,0:T(8,128)(2,1)}) %all-gather.5.cloned.1.call-update) | async-done | bytes 2359312 | tf_op jit(solution)/shard_map/all_gather | solution.py:51
  48.3 3.8 fusion.8
  52.2 31.3 %all-gather.9.cloned.1.call-done = bf16[2048,512]{1,0:T(8,128)(2,1)} async-done(((bf16[512,512]{1,0:T(8,128)(2,1)}), bf16[2048,512]{1,0:T(8,128)(2,1)}) %all-gather.9.cloned.1.call-update) | async-done | bytes 2097168 | tf_op jit(solution)/shard_map/all_gather | solution.py:58
  89.4 2.7 fusion.63
  100.2 2.8 fusion.101
  103.1 5.7 fusion.22
  110.7 593.1 %all-reduce.7.cloned.1.call-done = (f32[512,576]{1,0:T(8,128)}, f32[512,576]{1,0:T(8,128)}, f32[512,576]{1,0:T(8,128)}, f32[512,576]{1,0:T(8,128)}) async-done(((f32[512,576]{1,0:T(8,128)}, f32[512,576]{1,0:T(8,128)}, f32[512,576]{1,0:T(8,128)}, f32[512,576]{1,0:T(8,128)}), (f32[512,576]{1,0:T(8,128)}, f32[512,576]{1,0:T(8,128)}, f32[512,576]{1,0:T(8,128)}, ...) | async-done | bytes 4718608
  705.1 312.9 %reduce-scatter.3.cloned.1.call-done = f32[8,2304]{1,0:T(8,128)} async-done(((f32[512,2304]{1,0:T(8,128)}), f32[8,2304]{1,0:T(8,128)}) %reduce-scatter.3.cloned.1.call-update) | async-done | bytes 73744 | tf_op jit(solution)/shard_map/reduce_scatter | solution.py:60
  1019.6 2.6 copy.28
  1022.7 13.7 reduce.1
  1036.4 2.3 reshape.37
  1038.7 4.1 all-to-all-start
  1048.3 2.5 reshape.38
  1055.4 301.5 %all-gather.7.cloned.1.call-done = bf16[512,4,576]{2,1,0:T(4,128)(2,1)} async-done(((bf16[8,4,576]{2,1,0:T(4,128)(2,1)}), bf16[512,4,576]{2,1,0:T(4,128)(2,1)}) %all-gather.7.cloned.1.call-update) | async-done | bytes 2359312 | tf_op jit(solution)/shard_map/all_gather | solution.py:87
  1356.9 10.4 fusion.106
  1367.3 2.5 copy.37
  1369.8 2.5 fusion.17
  1372.3 2.5 copy.36
  1376.4 2.5 fusion.14
  1378.9 3.6 copy.35
  1386.0 2.5 fusion.15
  1388.5 3.6 copy.34
  1400.8 63.2 %reduce-scatter.5.cloned.1.call-done = bf16[1,512,512]{2,1,0:T(8,128)(2,1)} async-done(((bf16[4,512,512]{2,1,0:T(8,128)(2,1)}), bf16[1,512,512]{2,1,0:T(8,128)(2,1)}) %reduce-scatter.5.cloned.1.call-update) | async-done | bytes 524304 | tf_op jit(solution)/shard_map/reduce_scatter | solution.py:97
  (70 shorter events, 44.7 us)
Async XLA Ops:
  7.2 41.1 %copy-start = (bf16[1,2304,512]{2,1,0:T(8,128)(2,1)S(1)}, bf16[1,2304,512]{2,1,0:T(8,128)(2,1)}, u32[]{:S(2)}) copy-start(bf16[1,2304,512]{2,1,0:T(8,128)(2,1)} %param.14) | copy-start | bytes 7077892
  7.2 41.1 %copy-start.8 = (f32[1,512]{1,0:T(1,128)S(1)}, f32[1,512]{1,0:T(1,128)}, u32[]{:S(2)}) copy-start(f32[1,512]{1,0:T(1,128)} %param.15) | copy-start | bytes 6148
  7.2 41.1 %all-gather.5.cloned.1.call-start = ((), (), s32[]{:S(2)}) async-start(), calls=%async_computation.3 | async-start | bytes 2949120 | tf_op jit(solution)/shard_map/all_gather | solution.py:51
  11.5 71.9 %all-gather.9.cloned.1.call-start = ((), (), s32[]{:S(2)}) async-start(), calls=%async_computation.7 | async-start | bytes 2621440 | tf_op jit(solution)/shard_map/all_gather | solution.py:58
  52.1 651.6 %all-reduce.7.cloned.1.call-start = ((), (), s32[]{:S(2)}) async-start(), calls=%async_computation.8 | async-start | bytes 10485760
  83.5 10.4 slice-start
  85.4 4.0 copy-start.1
  87.4 6.4 slice-start.1
  100.2 2.9 copy-start.5
  100.2 917.9 %reduce-scatter.3.cloned.1.call-start = ((), (), s32[]{:S(2)}) async-start(), calls=%async_computation.4 | async-start | bytes 4792320 | tf_op jit(solution)/shard_map/reduce_scatter | solution.py:60
  108.8 0.7 copy-start.9
  1036.4 17.4 %copy-start.7 = (f32[4,576]{1,0:T(4,128)S(1)}, f32[4,576]{1,0:T(4,128)}, u32[]{:S(2)}) copy-start(f32[4,576]{1,0:T(4,128)} %param.17) | copy-start | bytes 27652
  1038.7 9.6 all-to-all-start
  1042.7 314.2 %all-gather.7.cloned.1.call-start = ((), (), s32[]{:S(2)}) async-start(), calls=%async_computation.5 | async-start | bytes 2662400 | tf_op jit(solution)/shard_map/all_gather | solution.py:87
  1055.3 408.7 %reduce-scatter.5.cloned.1.call-start = ((), (), s32[]{:S(2)}) async-start(), calls=%async_computation.6 | async-start | bytes 2621440 | tf_op jit(solution)/shard_map/reduce_scatter | solution.py:97
  1392.1 1.9 copy-start.2
  1397.4 1.8 copy-start.3
  1397.4 1.8 copy-start.4
  1397.4 1.8 copy-start.6
Sparse Core Ops, SparseCore 0:
  11.6 36.5 all-gather.4
  52.3 31.1 all-gather.8
  100.3 603.4 all-reduce.6
  706.2 311.8 reduce-scatter.2
  1055.4 301.3 all-gather.6
  1400.9 63.0 reduce-scatter.4
where the time goes:
time: 1470 us
  waiting for transfers between devices  1340 us (91%)
  matrix products  48.5 us (3%)
  local copies, waits for them, and re-layouts  40.8 us (3%)
  other arithmetic  22.6 us (2%)
  between operations  15 us (1%)
    unnamed x7, waiting for transfers between devices  593 us
    reduce_scatter x1, waiting for transfers between devices, body(): lax.psum_scatter(mlp_part, ('rows', 'feat'), scatter_dimension=0, tiled=T...  313 us
    all_gather x1, waiting for transfers between devices, body(): shard_rows = lax.all_gather(errors, ('rows', 'feat'), axis=0, tiled=True)  302 us
    reduce_scatter x1, waiting for transfers between devices, body(): lax.psum_scatter(gradients.astype(jnp.bfloat16), 'layer', scatter_dimensi...  63.2 us
    all_gather x1, waiting for transfers between devices, body(): whole = lax.all_gather(normed, 'rows', axis=0, tiled=True)  36.7 us
    all_gather x1, waiting for transfers between devices, body(): features_all = lax.all_gather(features[None], 'layer', axis=0, tiled=True)  31.3 us
  transfers between devices with their start and end apart: 7, of which 7 were waited for; matrix products, arithmetic and copies ran while one was open for 1% of the time, Pallas kernels for 0%

commit v1 on v0

v1 whole, which is shorter than its diff:
```python
import jax
import jax.numpy as jnp
from jax import lax
from jax.experimental import pallas as pl
from jax.experimental.pallas import tpu as pltpu
from jax.sharding import PartitionSpec as P

MESH = pl.DeviceIdType.MESH
BF16 = jnp.bfloat16
F32 = jnp.float32


def pair_index(source, target, layers=4):
    return source * layers - source * (source - 1) // 2 + target - source


def dot(left, right):
    return lax.dot_general(left, right, (((1,), (0,)), ((), ())), preferred_element_type=F32)


def dot_t(left, right):
    return lax.dot_general(left, right, (((1,), (1,)), ((), ())), preferred_element_type=F32)


def gelu(x):
    inner = 0.7978845608028654 * (x + 0.044715 * (x * x * x))
    return 0.5 * x * (1.0 + jnp.tanh(inner))


def kernel(
    resid, gain, gate_w, up_w, down_w, enc_w, enc_b, dec_w, dec_b,
    err_out, act_out,
    res_v, xg, ew, gw, uw, dw, wsend, wd, dv, fh,
    xs, own, xr, zf, zs, zr, ps, pr, ef, eg, acc, gs, ga, gt, gb,
    load_sem, w_ss, w_rs, xa_ss, xa_rs, zf_ss, zf_rs, fc_ss, fc_rs, fy_ss, fy_rs, ff_ss, ff_rs,
    x_ss, x_rs, z_ss, z_rs, p_ss, p_rs, az_ss, az_rs, ax_ss, ax_rs, gc_ss, gc_rs, gy_ss, gy_rs,
):
    l, r, f = lax.axis_index("layer"), lax.axis_index("rows"), lax.axis_index("feat")
    yh, c = l // 2, l % 2
    z, yl = f // 2, f % 2
    half = z % 2
    other = 1 - half

    def x_peer(d):
        return (l, (r + d) % 4, f)

    def z_peer(d):
        return (l, r, ((z + d) % 8) * 2 + yl)

    y_pair = (l, r, z * 2 + (1 - yl))
    core_l = yh * 2 + (1 - c)
    far_l = (1 - yh) * 2 + c
    cross_l = (1 - yh) * 2 + (1 - c)
    core_peer, far_peer, cross_peer = (core_l, r, f), (far_l, r, f), (cross_l, r, f)

    pending = []

    def send(src, dst, ss, rs, peer):
        copy = pltpu.make_async_remote_copy(
            src_ref=src, dst_ref=dst, send_sem=ss, recv_sem=rs, device_id=peer, device_id_type=MESH
        )
        copy.start()
        pending.append(copy)

    def arrived(dst, ss, rs):
        pltpu.make_async_remote_copy(
            src_ref=dst, dst_ref=dst, send_sem=ss, recv_sem=rs, device_id=core_peer, device_id_type=MESH
        ).wait_recv()

    loads = [
        pltpu.make_async_copy(src, dst, load_sem.at[i])
        for i, (src, dst) in enumerate(
            ((resid, res_v), (down_w, dw), (enc_w, ew), (gate_w, gw), (up_w, uw), (dec_w, dv))
        )
    ]
    for copy in loads:
        copy.start()
    barrier = pltpu.get_barrier_semaphore()
    peers = [x_peer(d) for d in (1, 2, 3)] + [z_peer(d) for d in range(1, 8)]
    peers += [y_pair, core_peer, far_peer, cross_peer]
    for peer in peers:
        pl.semaphore_signal(barrier, inc=1, device_id=peer, device_id_type=MESH)

    loads[0].wait()

    def norm_rows(i, carry):
        rows = pl.ds(pl.multiple_of(i * 16, 16), 16)
        value = res_v[rows, :].astype(F32)
        inv = lax.rsqrt(jnp.mean(value * value, axis=-1, keepdims=True) + 1e-06)
        out = (value * inv * gain[...]).astype(BF16)
        xg[0, r, rows, :] = out[:, :1152]
        xg[1, r, rows, :] = out[:, 1152:]
        return carry

    lax.fori_loop(0, 8, norm_rows, 0)
    pl.semaphore_wait(barrier, len(peers))
    for d in (1, 3, 2):
        send(xg.at[half, r], xg.at[half, r], xa_ss.at[d - 1], xa_rs.at[d - 1], x_peer(d))

    loads[1].wait()
    for q in range(4):
        wsend[q] = dw[:, q * 576 : (q + 1) * 576]
    for i, (peer_l, peer) in enumerate(((core_l, core_peer), (far_l, far_peer), (cross_l, cross_peer))):
        send(wsend.at[peer_l], wd.at[l], w_ss.at[i], w_rs.at[i], peer)
    wd[l] = wsend[l]

    for copy in loads[2:5]:
        copy.wait()

    def features(chunk):
        left, right = xg[0, chunk], xg[1, chunk]
        pre = dot(left, ew[:1152]) + dot(right, ew[1152:]) + enc_b[...]
        fh[l, chunk, :, :512] = jnp.maximum(pre, 0.0).astype(BF16)
        gate = dot_t(left, gw[:, :1152]) + dot_t(right, gw[:, 1152:])
        up = dot_t(left, uw[:, :1152]) + dot_t(right, uw[:, 1152:])
        fh[l, chunk, :, 512:] = (gelu(gate) * up).astype(BF16)

    def share(d):
        chunk = (r - d) % 4
        features(chunk)
        send(fh.at[l, chunk], fh.at[l, chunk], fy_ss.at[d], fy_rs.at[d], far_peer)
        send(fh.at[l, chunk], fh.at[l, chunk], fc_ss.at[d], fc_rs.at[d], core_peer)

    def hand_on(d):
        chunk = (r - d) % 4
        arrived(fh.at[far_l, chunk], fy_ss.at[d], fy_rs.at[d])
        send(fh.at[far_l, chunk], fh.at[far_l, chunk], ff_ss.at[d], ff_rs.at[d], core_peer)

    def have(d):
        chunk = (r - d) % 4
        arrived(fh.at[core_l, chunk], fc_ss.at[d], fc_rs.at[d])
        arrived(fh.at[cross_l, chunk], ff_ss.at[d], ff_rs.at[d])

    low, high = pl.ds(0, 64), pl.ds(64, 64)

    def relay(d):
        chunk = (r - d) % 4
        arrived(xg.at[half, chunk], xa_ss.at[d - 1], xa_rs.at[d - 1])
        send(xg.at[half, chunk, low], xg.at[half, chunk, low], zf_ss.at[d - 1, 0], zf_rs.at[d - 1, 0], z_peer(1))
        send(xg.at[half, chunk, high], xg.at[half, chunk, high], zf_ss.at[d - 1, 1], zf_rs.at[d - 1, 1], z_peer(7))

    def rest(d):
        chunk = (r - d) % 4
        arrived(xg.at[other, chunk, low], zf_ss.at[d - 1, 0], zf_rs.at[d - 1, 0])
        arrived(xg.at[other, chunk, high], zf_ss.at[d - 1, 1], zf_rs.at[d - 1, 1])

    share(0)
    relay(1)
    relay(3)
    rest(1)
    share(1)
    relay(2)
    hand_on(0)
    rest(3)
    share(3)
    hand_on(1)
    rest(2)
    share(2)
    hand_on(3)
    hand_on(2)
    loads[5].wait()
    for i, peer_l in enumerate((core_l, far_l, cross_l)):
        arrived(wd.at[peer_l], w_ss.at[i], w_rs.at[i])
    for d in (0, 1, 3, 2):
        have(d)

    def partial_sum(t, chunk):
        total = -dot(fh[t, chunk, :, 512:], wd[t])
        for s in range(t + 1):
            total = total + dot_t(fh[s, chunk, :, :512], dv[pair_index(s, t)])
        return total

    def decode(t):
        for d in (2, 1, 3):
            chunk = (r + d) % 4
            xs[t, chunk] = partial_sum(t, chunk).astype(BF16)
            send(xs.at[t, chunk], xr.at[t, d - 1], x_ss.at[t, d - 1], x_rs.at[t, d - 1], x_peer(d))
        own[t] = partial_sum(t, r)

    def sum_x(t):
        for d in (1, 3, 2):
            arrived(xr.at[t, d - 1], x_ss.at[t, d - 1], x_rs.at[t, d - 1])

        def block(i, carry):
            rows = pl.ds(pl.multiple_of(i * 16, 16), 16)
            value = own[t, rows, :]
            for d in range(3):
                value = value + xr[t, d, rows, :].astype(F32)
            zf[t, i] = value
            zs[t, i] = value.astype(BF16)
            return carry

        lax.fori_loop(0, 8, block, 0)
        for d in (4, 3, 5, 2, 6, 1, 7):
            to = (z + d) % 8
            send(zs.at[t, to], zr.at[t, d - 1], z_ss.at[t, d - 1], z_rs.at[t, d - 1], z_peer(d))

    def sum_z(t):
        for d in range(1, 8):
            arrived(zr.at[t, d - 1], z_ss.at[t, d - 1], z_rs.at[t, d - 1])
        value = zf[t, z]
        for d in range(7):
            value = value + zr[t, d].astype(F32)
        ps[t] = value.astype(BF16)
        send(ps.at[t], pr.at[t], p_ss.at[t], p_rs.at[t], y_pair)

    def sum_pair(t):
        arrived(pr.at[t], p_ss.at[t], p_rs.at[t])
        value = ps[t].astype(F32) + pr[t].astype(F32) + dec_b[t : t + 1, :]
        ef[t] = value
        eg[t, r, z] = value.astype(BF16)
        err_out[t] = ef[t, pl.ds(pl.multiple_of(yl * 8, 8), 8), :].astype(BF16)
        for d in (4, 3, 5, 2, 6, 1, 7):
            send(eg.at[t, r, z], eg.at[t, r, z], az_ss.at[t, d - 1], az_rs.at[t, d - 1], z_peer(d))

    def gather_z(t):
        for d in range(1, 8):
            arrived(eg.at[t, r, (z - d) % 8], az_ss.at[t, d - 1], az_rs.at[t, d - 1])
        for d in (2, 1, 3):
            send(eg.at[t, r], eg.at[t, r], ax_ss.at[t, d - 1], ax_rs.at[t, d - 1], x_peer(d))

    def gradient(t):
        for d in (0, 1, 3, 2):
            chunk = (r - d) % 4
            if d:
                arrived(eg.at[t, chunk], ax_ss.at[t, d - 1], ax_rs.at[t, d - 1])
            errors = eg[t, chunk].reshape(128, 576)
            rows = pl.ds(pl.multiple_of(chunk * 128, 128), 128)
            for s in range(t, -1, -1):
                value = dot(errors, dv[pair_index(s, t)])
                if t < 3:
                    value = value + acc[s, rows, :]
                acc[s, rows, :] = value
                if s == t:
                    gs[s, rows, :] = value.astype(BF16)

    def core_send(s):
        @pl.when(c != s % 2)
        def _():
            pltpu.make_async_remote_copy(
                src_ref=gs.at[s], dst_ref=ga.at[s], send_sem=gc_ss.at[s], recv_sem=gc_rs.at[s],
                device_id=core_peer, device_id_type=MESH,
            ).start()

    def far_copy(s):
        return pltpu.make_async_remote_copy(
            src_ref=gt.at[s], dst_ref=gb, send_sem=gy_ss.at[s], recv_sem=gy_rs.at[s],
            device_id=far_peer, device_id_type=MESH,
        )

    def core_sum(s):
        @pl.when(c == s % 2)
        def _():
            arrived(ga.at[s], gc_ss.at[s], gc_rs.at[s])

            def block(i, carry):
                rows = pl.ds(pl.multiple_of(i * 32, 32), 32)
                value = acc[s, rows, :] + ga[s, rows, :].astype(F32)
                acc[s, rows, :] = value
                gt[s, rows, :] = value.astype(BF16)
                return carry

            lax.fori_loop(0, 16, block, 0)

            @pl.when(yh != s // 2)
            def _():
                far_copy(s).start()

    def finish(s):
        @pl.when(l == s)
        def _():
            far_copy(s).wait_recv()

            def block(i, carry):
                rows = pl.ds(pl.multiple_of(i * 32, 32), 32)
                act_out[rows, :] = (acc[s, rows, :] + gb[rows, :].astype(F32)).astype(BF16)
                return carry

            lax.fori_loop(0, 16, block, 0)

        @pl.when(c != s % 2)
        def _():
            pltpu.make_async_remote_copy(
                src_ref=gs.at[s], dst_ref=ga.at[s], send_sem=gc_ss.at[s], recv_sem=gc_rs.at[s],
                device_id=core_peer, device_id_type=MESH,
            ).wait_send()

        @pl.when((c == s % 2) & (yh != s // 2))
        def _():
            far_copy(s).wait_send()

    for t in (3, 2, 1, 0):
        decode(t)
    sum_x(3)
    sum_z(3)
    sum_pair(3)
    sum_x(2)
    gather_z(3)
    sum_z(2)
    sum_pair(2)
    sum_x(1)
    gather_z(2)
    sum_z(1)
    sum_pair(1)
    sum_x(0)
    gather_z(1)
    sum_z(0)
    sum_pair(0)
    gradient(3)
    core_send(3)
    gather_z(0)
    gradient(2)
    core_send(2)
    core_sum(3)
    gradient(1)
    core_send(1)
    core_sum(2)
    gradient(0)
    core_send(0)
    core_sum(1)
    core_sum(0)
    for s in (3, 2, 1, 0):
        finish(s)
    for copy in pending:
        copy.wait_send()


def body(resid, norm_gain, gate_weight, up_weight, down_weight, enc_weight, enc_bias, dec_weight, dec_bias):
    any_spec = pl.BlockSpec(memory_space=pl.ANY)
    vmem_spec = pl.BlockSpec(memory_space=pltpu.VMEM)
    vmem = pltpu.VMEM
    dma = pltpu.SemaphoreType.DMA
    scratch = [
        vmem((128, 2304), BF16),
        vmem((2, 4, 128, 1152), BF16),
        vmem((2304, 512), BF16),
        vmem((144, 2304), BF16),
        vmem((144, 2304), BF16),
        vmem((144, 2304), BF16),
        vmem((4, 144, 576), BF16),
        vmem((4, 144, 576), BF16),
        vmem((10, 576, 512), BF16),
        vmem((4, 4, 128, 656), BF16),
        vmem((4, 4, 128, 576), BF16),
        vmem((4, 128, 576), F32),
        vmem((4, 3, 128, 576), BF16),
        vmem((4, 8, 16, 576), F32),
        vmem((4, 8, 16, 576), BF16),
        vmem((4, 7, 16, 576), BF16),
        vmem((4, 16, 576), BF16),
        vmem((4, 16, 576), BF16),
        vmem((4, 16, 576), F32),
        vmem((4, 4, 8, 16, 576), BF16),
        vmem((4, 512, 512), F32),
        vmem((4, 512, 512), BF16),
        vmem((4, 512, 512), BF16),
        vmem((4, 512, 512), BF16),
        vmem((512, 512), BF16),
        dma((6,)),
    ]
    for shape in ((3,), (3,), (3, 2), (4,), (4,), (4,), (4, 3), (4, 7), (4,), (4, 7), (4, 3), (4,), (4,)):
        scratch += [dma(shape), dma(shape)]
    errors, act_grad = pl.pallas_call(
        kernel,
        out_shape=(
            jax.ShapeDtypeStruct((4, 8, 576), BF16),
            jax.ShapeDtypeStruct((512, 512), BF16),
        ),
        in_specs=[any_spec, vmem_spec, any_spec, any_spec, any_spec, any_spec, vmem_spec, any_spec, vmem_spec],
        out_specs=(vmem_spec, vmem_spec),
        scratch_shapes=scratch,
        compiler_params=pltpu.CompilerParams(
            collective_id=1, has_side_effects=True, vmem_limit_bytes=60 * 2**20
        ),
        cost_estimate=pl.CostEstimate(flops=8_200_000_000, bytes_accessed=12_000_000, transcendentals=100_000),
    )(
        resid[0], norm_gain, gate_weight[0], up_weight[0], down_weight[0], enc_weight[0], enc_bias,
        jnp.swapaxes(dec_weight, 1, 2), dec_bias,
    )
    return jnp.transpose(errors, (1, 0, 2)), act_grad[None]


def solution(mesh):
    in_specs = (
        P("layer", "rows", None),
        P("layer", None),
        P("layer", ("rows", "feat"), None),
        P("layer", ("rows", "feat"), None),
        P("layer", ("rows", "feat"), None),
        P("layer", None, ("rows", "feat")),
        P("layer", ("rows", "feat")),
        P(None, ("rows", "feat"), "layer"),
        P(None, "layer"),
    )
    out_specs = (P(("rows", "feat"), None, "layer"), P("layer", None, ("rows", "feat")))
    return jax.shard_map(body, mesh=mesh, in_specs=in_specs, out_specs=out_specs, check_vma=False)
```

time: 1470 us -> 127 us (0.09)
  waiting for transfers between devices: 1340 us -> 0 us
  Pallas kernels: 0 us -> 122 us
  matrix products: 48.5 us -> 0 us
  local copies, waits for them, and re-layouts: 40.8 us -> 3.28 us
  other arithmetic: 22.6 us -> 0 us
    unnamed x7 -> x0, waiting for transfers between devices: 593 us -> none
    reduce_scatter x2 -> x0, waiting for transfers between devices: 376 us -> none  [the longest x1 313 us: body(): lax.psum_scatter(mlp_part, ('rows', 'feat'), scatter_dimension=0, tiled=T...]
    all_gather x3 -> x0, waiting for transfers between devices: 369 us -> none  [the longest x1 302 us: body(): shard_rows = lax.all_gather(errors, ('rows', 'feat'), axis=0, tiled=True)]
    pallas_call x0 -> x1, Pallas kernels: none -> 122 us  [body(): pl.pallas_call(kernel, out_shape=(jax.ShapeDtypeStruct((4, 8, 576), BF16)...]
    dot_general x23 -> x0, matrix products: 48.5 us -> none  [the longest x11 22.4 us: contract_last(): lax.dot_general(left, right, (((1,), (1,)), ((), ())), preferred_element_...]
    unnamed x34 -> x2, local copies, waits for them, and re-layouts: 20.9 us -> 3.28 us
  transfers between devices with their start and end apart: 7 -> 0, of which waited for: 7 -> 0; matrix products, arithmetic and copies ran while one was open for 1% -> 0% of each run, Pallas kernels for 0% -> 0%
where the time goes in v1:
time: 127 us; the launch traced here: 126 us
  Pallas kernels  122 us (96%)
  local copies, waits for them, and re-layouts  3.28 us (3%)
    pallas_call x1, Pallas kernels, body(): pl.pallas_call(kernel, out_shape=(jax.ShapeDtypeStruct((4, 8, 576), BF16)...  122 us
    unnamed x2, local copies, waits for them, and re-layouts  3.28 us

profile of v1, /device:TPU:6, one launch (start us, length us, event | category | flops | bytes accessed | tf_op | source)
XLA Modules:
  0.0 126.3 jit_solution(8109166546786321706)
XLA Ops:
  0.6 122.4 %shard_map.104 = (bf16[4,8,576]{2,1,0:T(8,128)(2,1)}, bf16[512,512]{1,0:T(8,128)(2,1)}) custom-call(bf16[128,2304]{1,0:T(8,128)(2,1)} %bitcast.15, f32[1,2304]{1,0:T(1,128)} %gain.1, bf16[144,2304]{1,0:T(8,128)(2,1)} %bitcast.12, bf16[144,2304]{1,0:T(8,128)(2,1)} %bitcast.13, bf16[144,2304]{1,0:T(8,128)(2,1)} %bitcast.14, bf16[2304,512]{1,0:T(8,128)(2,1)} %bitcast.11, ...), custom_call_target="tpu_custom_call" | custom-call | flops 8200000000 | bytes 12000000 | tf_op jit(solution)/shard_map/pallas_call | solution.py:363
  123.1 1.4 %copy.11 = bf16[8,4,576]{2,1,0:T(4,128)(2,1)} copy(bf16[8,4,576]{2,0,1:T(8,128)(2,1)} %bitcast.9) | data formatting | bytes 73728
  124.5 1.9 %copy.13 = bf16[1,512,512]{2,1,0:T(8,128)(2,1)} copy(bf16[1,512,512]{2,1,0:T(8,128)(2,1)} %bitcast.8) | data formatting | bytes 1048576

commit v2 on v1

--- a/solution.py
+++ b/solution.py
@@ -8,6 +8,8 @@
 MESH = pl.DeviceIdType.MESH
 BF16 = jnp.bfloat16
 F32 = jnp.float32
+DIRECT_Z = (3, 0)
+DIRECT_X = (0,)
 
 
 def pair_index(source, target, layers=4):
@@ -32,8 +34,8 @@
     err_out, act_out,
     res_v, xg, ew, gw, uw, dw, wsend, wd, dv, fh,
     xs, own, xr, zf, zs, zr, ps, pr, ef, eg, acc, gs, ga, gt, gb,
-    load_sem, w_ss, w_rs, xa_ss, xa_rs, zf_ss, zf_rs, fc_ss, fc_rs, fy_ss, fy_rs, ff_ss, ff_rs,
-    x_ss, x_rs, z_ss, z_rs, p_ss, p_rs, az_ss, az_rs, ax_ss, ax_rs, gc_ss, gc_rs, gy_ss, gy_rs,
+    load_sem, w_ss, w_rs, xa_ss, xa_rs, xb_ss, xb_rs, zf_ss, zf_rs, fc_ss, fc_rs, fy_ss, fy_rs, ff_ss, ff_rs,
+    x_ss, x_rs, z_ss, z_rs, p_ss, p_rs, az_ss, az_rs, ax_ss, ax_rs, ay_ss, ay_rs, gc_ss, gc_rs, gy_ss, gy_rs,
 ):
     l, r, f = lax.axis_index("layer"), lax.axis_index("rows"), lax.axis_index("feat")
     yh, c = l // 2, l % 2
@@ -94,7 +96,7 @@
 
     lax.fori_loop(0, 8, norm_rows, 0)
     pl.semaphore_wait(barrier, len(peers))
-    for d in (1, 3, 2):
+    for d in (1, 3):
         send(xg.at[half, r], xg.at[half, r], xa_ss.at[d - 1], xa_rs.at[d - 1], x_peer(d))
 
     loads[1].wait()
@@ -135,34 +137,22 @@
 
     def relay(d):
         chunk = (r - d) % 4
-        arrived(xg.at[half, chunk], xa_ss.at[d - 1], xa_rs.at[d - 1])
-        send(xg.at[half, chunk, low], xg.at[half, chunk, low], zf_ss.at[d - 1, 0], zf_rs.at[d - 1, 0], z_peer(1))
-        send(xg.at[half, chunk, high], xg.at[half, chunk, high], zf_ss.at[d - 1, 1], zf_rs.at[d - 1, 1], z_peer(7))
+        parts = ((low, 1, 0, 1), (high, 3, 1, 7))
+        if d != 2:
+            arrived(xg.at[half, chunk], xa_ss.at[d - 1], xa_rs.at[d - 1])
+            part, step, slot, _ = parts[d // 2]
+            piece = xg.at[half, chunk, part]
+            send(piece, piece, xb_ss.at[slot], xb_rs.at[slot], x_peer(step))
+        for part, _, slot, z_step in parts:
+            piece = xg.at[half, chunk, part]
+            if d == 2:
+                arrived(piece, xb_ss.at[slot], xb_rs.at[slot])
+            send(piece, piece, zf_ss.at[d - 1, slot], zf_rs.at[d - 1, slot], z_peer(z_step))
 
     def rest(d):
         chunk = (r - d) % 4
         arrived(xg.at[other, chunk, low], zf_ss.at[d - 1, 0], zf_rs.at[d - 1, 0])
         arrived(xg.at[other, chunk, high], zf_ss.at[d - 1, 1], zf_rs.at[d - 1, 1])
-
-    share(0)
-    relay(1)
-    relay(3)
-    rest(1)
-    share(1)
-    relay(2)
-    hand_on(0)
-    rest(3)
-    share(3)
-    hand_on(1)
-    rest(2)
-    share(2)
-    hand_on(3)
-    hand_on(2)
-    loads[5].wait()
-    for i, peer_l in enumerate((core_l, far_l, cross_l)):
-        arrived(wd.at[peer_l], w_ss.at[i], w_rs.at[i])
-    for d in (0, 1, 3, 2):
-        have(d)
 
     def partial_sum(t, chunk):
         total = -dot(fh[t, chunk, :, 512:], wd[t])
@@ -170,12 +160,14 @@
             total = total + dot_t(fh[s, chunk, :, :512], dv[pair_index(s, t)])
         return total
 
-    def decode(t):
-        for d in (2, 1, 3):
-            chunk = (r + d) % 4
-            xs[t, chunk] = partial_sum(t, chunk).astype(BF16)
-            send(xs.at[t, chunk], xr.at[t, d - 1], x_ss.at[t, d - 1], x_rs.at[t, d - 1], x_peer(d))
-        own[t] = partial_sum(t, r)
+    def decode(d, targets):
+        chunk = (r - d) % 4
+        for t in targets:
+            if d:
+                xs[t, d - 1] = partial_sum(t, chunk).astype(BF16)
+                send(xs.at[t, d - 1], xr.at[t, d - 1], x_ss.at[t, d - 1], x_rs.at[t, d - 1], x_peer(4 - d))
+            else:
+                own[t] = partial_sum(t, chunk)
 
     def sum_x(t):
         for d in (1, 3, 2):
@@ -204,125 +196,196 @@
         ps[t] = value.astype(BF16)
         send(ps.at[t], pr.at[t], p_ss.at[t], p_rs.at[t], y_pair)
 
+    def send_z(t, origin, step, distance):
+        piece = eg.at[t, r, (z - origin) % 8]
+        send(piece, piece, az_ss.at[t, distance - 1], az_rs.at[t, distance - 1], z_peer(step))
+
+    def arrived_z(t, d):
+        arrived(eg.at[t, r, (z - d) % 8], az_ss.at[t, d - 1], az_rs.at[t, d - 1])
+
+    def relay_z(t):
+        arrived_z(t, 2)
+        if t % 2 == 0:
+            send_z(t, 2, 2, 4)
+        send_z(t, 2, 1, 3)
+        arrived_z(t, 6)
+        if t % 2 == 1:
+            send_z(t, 6, 6, 4)
+        send_z(t, 6, 7, 5)
+
     def sum_pair(t):
         arrived(pr.at[t], p_ss.at[t], p_rs.at[t])
         value = ps[t].astype(F32) + pr[t].astype(F32) + dec_b[t : t + 1, :]
         ef[t] = value
         eg[t, r, z] = value.astype(BF16)
         err_out[t] = ef[t, pl.ds(pl.multiple_of(yl * 8, 8), 8), :].astype(BF16)
-        for d in (4, 3, 5, 2, 6, 1, 7):
-            send(eg.at[t, r, z], eg.at[t, r, z], az_ss.at[t, d - 1], az_rs.at[t, d - 1], z_peer(d))
+        for d in (4, 3, 5, 2, 6, 1, 7) if t in DIRECT_Z else (2, 6, 1, 7):
+            send_z(t, 0, d, d)
 
     def gather_z(t):
-        for d in range(1, 8):
-            arrived(eg.at[t, r, (z - d) % 8], az_ss.at[t, d - 1], az_rs.at[t, d - 1])
-        for d in (2, 1, 3):
+        for d in (1, 2, 3, 4, 5, 6, 7) if t in DIRECT_Z else (1, 3, 4, 5, 7):
+            arrived_z(t, d)
+        for d in (2, 1, 3) if t in DIRECT_X else (1, 3):
             send(eg.at[t, r], eg.at[t, r], ax_ss.at[t, d - 1], ax_rs.at[t, d - 1], x_peer(d))
 
-    def gradient(t):
-        for d in (0, 1, 3, 2):
+    first_z, last_z = pl.ds(0, 4), pl.ds(4, 4)
+
+    def pass_on(t):
+        for d, part, slot in ((1, first_z, 0), (3, last_z, 1)):
             chunk = (r - d) % 4
-            if d:
-                arrived(eg.at[t, chunk], ax_ss.at[t, d - 1], ax_rs.at[t, d - 1])
-            errors = eg[t, chunk].reshape(128, 576)
-            rows = pl.ds(pl.multiple_of(chunk * 128, 128), 128)
-            for s in range(t, -1, -1):
-                value = dot(errors, dv[pair_index(s, t)])
-                if t < 3:
-                    value = value + acc[s, rows, :]
-                acc[s, rows, :] = value
-                if s == t:
-                    gs[s, rows, :] = value.astype(BF16)
-
-    def core_send(s):
+            arrived(eg.at[t, chunk], ax_ss.at[t, d - 1], ax_rs.at[t, d - 1])
+            piece = eg.at[t, chunk, part]
+            send(piece, piece, ay_ss.at[t, slot], ay_rs.at[t, slot], x_peer(d))
+
+    def gradient(t, d):
+        chunk = (r - d) % 4
+        if d == 2:
+            if t in DIRECT_X:
+                arrived(eg.at[t, chunk], ax_ss.at[t, 1], ax_rs.at[t, 1])
+            for part, slot in () if t in DIRECT_X else ((first_z, 0), (last_z, 1)):
+                arrived(eg.at[t, chunk, part], ay_ss.at[t, slot], ay_rs.at[t, slot])
+        elif d and t in DIRECT_X:
+            arrived(eg.at[t, chunk], ax_ss.at[t, d - 1], ax_rs.at[t, d - 1])
+        errors = eg[t, chunk].reshape(128, 576)
+        for s in range(t, -1, -1):
+            value = dot(errors, dv[pair_index(s, t)])
+            if t < 3:
+                value = value + acc[s, d]
+            acc[s, d] = value
+            if s == t:
+                gs[s, d] = value.astype(BF16)
+
+    def core_copy(s, d):
+        return pltpu.make_async_remote_copy(
+            src_ref=gs.at[s, d], dst_ref=ga.at[s, d], send_sem=gc_ss.at[s, d], recv_sem=gc_rs.at[s, d],
+            device_id=core_peer, device_id_type=MESH,
+        )
+
+    def far_copy(s, d):
+        return pltpu.make_async_remote_copy(
+            src_ref=gt.at[s, d], dst_ref=gb.at[d], send_sem=gy_ss.at[s, d], recv_sem=gy_rs.at[s, d],
+            device_id=far_peer, device_id_type=MESH,
+        )
+
+    def core_send(s, d):
         @pl.when(c != s % 2)
         def _():
-            pltpu.make_async_remote_copy(
-                src_ref=gs.at[s], dst_ref=ga.at[s], send_sem=gc_ss.at[s], recv_sem=gc_rs.at[s],
-                device_id=core_peer, device_id_type=MESH,
-            ).start()
-
-    def far_copy(s):
-        return pltpu.make_async_remote_copy(
-            src_ref=gt.at[s], dst_ref=gb, send_sem=gy_ss.at[s], recv_sem=gy_rs.at[s],
-            device_id=far_peer, device_id_type=MESH,
-        )
-
-    def core_sum(s):
+            core_copy(s, d).start()
+
+    def core_sum(s, d):
         @pl.when(c == s % 2)
         def _():
-            arrived(ga.at[s], gc_ss.at[s], gc_rs.at[s])
-
-            def block(i, carry):
-                rows = pl.ds(pl.multiple_of(i * 32, 32), 32)
-                value = acc[s, rows, :] + ga[s, rows, :].astype(F32)
-                acc[s, rows, :] = value
-                gt[s, rows, :] = value.astype(BF16)
-                return carry
-
-            lax.fori_loop(0, 16, block, 0)
+            core_copy(s, d).wait_recv()
+            value = acc[s, d] + ga[s, d].astype(F32)
+            acc[s, d] = value
+            gt[s, d] = value.astype(BF16)
 
             @pl.when(yh != s // 2)
             def _():
-                far_copy(s).start()
-
-    def finish(s):
+                far_copy(s, d).start()
+
+    def finish(s, d):
         @pl.when(l == s)
         def _():
-            far_copy(s).wait_recv()
-
-            def block(i, carry):
-                rows = pl.ds(pl.multiple_of(i * 32, 32), 32)
-                act_out[rows, :] = (acc[s, rows, :] + gb[rows, :].astype(F32)).astype(BF16)
-                return carry
-
-            lax.fori_loop(0, 16, block, 0)
+            far_copy(s, d).wait_recv()
+            rows = pl.ds(pl.multiple_of(((r - d) % 4) * 128, 128), 128)
+            act_out[rows, :] = (acc[s, d] + gb[d].astype(F32)).astype(BF16)
 
         @pl.when(c != s % 2)
         def _():
-            pltpu.make_async_remote_copy(
-                src_ref=gs.at[s], dst_ref=ga.at[s], send_sem=gc_ss.at[s], recv_sem=gc_rs.at[s],
-                device_id=core_peer, device_id_type=MESH,
-            ).wait_send()
+            core_copy(s, d).wait_send()
 
         @pl.when((c == s % 2) & (yh != s // 2))
         def _():
-            far_copy(s).wait_send()
-
-    for t in (3, 2, 1, 0):
-        decode(t)
+            far_copy(s, d).wait_send()
+
+    share(0)
+    relay(1)
+    relay(3)
+    rest(1)
+    share(1)
+    hand_on(0)
+    relay(2)
+    rest(3)
+    share(3)
+    rest(2)
+    share(2)
+    hand_on(1)
+    loads[5].wait()
+    for i, peer_l in enumerate((core_l, far_l, cross_l)):
+        arrived(wd.at[peer_l], w_ss.at[i], w_rs.at[i])
+    have(0)
+    decode(0, (3, 2))
+    hand_on(3)
+    have(1)
+    decode(1, (3, 2))
+    have(3)
+    decode(3, (3, 2))
+    hand_on(2)
+    have(2)
+    decode(2, (3, 2))
+    decode(1, (1, 0))
+    decode(3, (1, 0))
+    decode(2, (1, 0))
+    decode(0, (1, 0))
     sum_x(3)
+    sum_x(2)
     sum_z(3)
     sum_pair(3)
-    sum_x(2)
-    gather_z(3)
     sum_z(2)
     sum_pair(2)
+    gather_z(3)
+    relay_z(2)
     sum_x(1)
     gather_z(2)
+    sum_x(0)
     sum_z(1)
     sum_pair(1)
-    sum_x(0)
+    pass_on(3)
+    sum_z(0)
+    relay_z(1)
+    sum_pair(0)
     gather_z(1)
-    sum_z(0)
-    sum_pair(0)
-    gradient(3)
-    core_send(3)
+    pass_on(2)
     gather_z(0)
-    gradient(2)
-    core_send(2)
-    core_sum(3)
-    gradient(1)
-    core_send(1)
-    core_sum(2)
-    gradient(0)
-    core_send(0)
-    core_sum(1)
-    core_sum(0)
+    order = (0, 1, 3, 2)
+
+    def step(t, d):
+        gradient(t, d)
+        core_send(t, d)
+
+    step(3, 0)
+    step(3, 1)
+    step(3, 3)
+    pass_on(1)
+    step(3, 2)
+    step(2, 0)
+    core_sum(3, 0)
+    step(2, 1)
+    core_sum(3, 1)
+    step(2, 3)
+    core_sum(3, 3)
+    step(2, 2)
+    core_sum(3, 2)
+    for d in order:
+        step(1, d)
+        core_sum(2, d)
+    for i, d in enumerate(order):
+        step(0, d)
+        core_sum(1, d)
+        if i:
+            core_sum(0, order[i - 1])
+    core_sum(0, 2)
     for s in (3, 2, 1, 0):
-        finish(s)
+        for d in order:
+            finish(s, d)
     for copy in pending:
         copy.wait_send()
+
+
+def write_out(errors, grads, err_out, act_out):
+    err_out[...] = jnp.stack([errors[t].astype(F32) for t in range(4)], axis=1).astype(BF16)
+    act_out[...] = grads[...]
 
 
 def body(resid, norm_gain, gate_weight, up_weight, down_weight, enc_weight, enc_bias, dec_weight, dec_bias):
@@ -341,7 +404,7 @@
         vmem((4, 144, 576), BF16),
         vmem((10, 576, 512), BF16),
         vmem((4, 4, 128, 656), BF16),
-        vmem((4, 4, 128, 576), BF16),
+        vmem((4, 3, 128, 576), BF16),
         vmem((4, 128, 576), F32),
         vmem((4, 3, 128, 576), BF16),
         vmem((4, 8, 16, 576), F32),
@@ -351,14 +414,14 @@
         vmem((4, 16, 576), BF16),
         vmem((4, 16, 576), F32),
         vmem((4, 4, 8, 16, 576), BF16),
-        vmem((4, 512, 512), F32),
-        vmem((4, 512, 512), BF16),
-        vmem((4, 512, 512), BF16),
-        vmem((4, 512, 512), BF16),
-        vmem((512, 512), BF16),
+        vmem((4, 4, 128, 512), F32),
+        vmem((4, 4, 128, 512), BF16),
+        vmem((4, 4, 128, 512), BF16),
+        vmem((4, 4, 128, 512), BF16),
+        vmem((4, 128, 512), BF16),
         dma((6,)),
     ]
-    for shape in ((3,), (3,), (3, 2), (4,), (4,), (4,), (4, 3), (4, 7), (4,), (4, 7), (4, 3), (4,), (4,)):
+    for shape in ((3,), (3,), (2,), (3, 2), (4,), (4,), (4,), (4, 3), (4, 7), (4,), (4, 7), (4, 3), (4, 2), (4, 4), (4, 4)):
         scratch += [dma(shape), dma(shape)]
     errors, act_grad = pl.pallas_call(
         kernel,
@@ -377,7 +440,12 @@
         resid[0], norm_gain, gate_weight[0], up_weight[0], down_weight[0], enc_weight[0], enc_bias,
         jnp.swapaxes(dec_weight, 1, 2), dec_bias,
     )
-    return jnp.transpose(errors, (1, 0, 2)), act_grad[None]
+    return pl.pallas_call(
+        write_out,
+        out_shape=(jax.ShapeDtypeStruct((8, 4, 576), BF16), jax.ShapeDtypeStruct((1, 512, 512), BF16)),
+        in_specs=[vmem_spec, vmem_spec],
+        out_specs=(vmem_spec, vmem_spec),
+    )(errors, act_grad[None])
 
 
 def solution(mesh):

time: 127 us -> 116 us (0.913)
  Pallas kernels: 122 us -> 116 us
  local copies, waits for them, and re-layouts: 3.28 us -> 0 us
    pallas_call x1, Pallas kernels: 122 us -> 114 us  [body(): pl.pallas_call(kernel, out_shape=(jax.ShapeDtypeStruct((4, 8, 576), BF16)...]
    unnamed x2 -> x0, local copies, waits for them, and re-layouts: 3.28 us -> none
    pallas_call x0 -> x1, Pallas kernels: none -> 1.91 us  [body(): pl.pallas_call(write_out, out_shape=(jax.ShapeDtypeStruct((8, 4, 576), BF...]
where the time goes in v2:
time: 116 us
  Pallas kernels  116 us (100%)
    pallas_call x1, Pallas kernels, body(): pl.pallas_call(kernel, out_shape=(jax.ShapeDtypeStruct((4, 8, 576), BF16)...  114 us

profile of v2, /device:TPU:6, one launch (start us, length us, event | category | flops | bytes accessed | tf_op | source)
XLA Modules:
  0.0 116.3 jit_solution(1305225435460947123)
XLA Ops:
  0.6 113.7 %shard_map.104 = (bf16[4,8,576]{2,1,0:T(8,128)(2,1)}, bf16[512,512]{1,0:T(8,128)(2,1)}) custom-call(bf16[128,2304]{1,0:T(8,128)(2,1)} %bitcast.13, f32[1,2304]{1,0:T(1,128)} %gain.1, bf16[144,2304]{1,0:T(8,128)(2,1)} %bitcast.10, bf16[144,2304]{1,0:T(8,128)(2,1)} %bitcast.11, bf16[144,2304]{1,0:T(8,128)(2,1)} %bitcast.12, bf16[2304,512]{1,0:T(8,128)(2,1)} %bitcast.9, ...), custom_call_target="tpu_custom_call" | custom-call | flops 8200000000 | bytes 12000000 | tf_op jit(solution)/shard_map/pallas_call | solution.py:426
  114.4 1.9 %shard_map.105 = (bf16[8,4,576]{2,1,0:T(4,128)(2,1)}, bf16[1,512,512]{2,1,0:T(8,128)(2,1)}) custom-call(bf16[4,8,576]{2,1,0:T(8,128)(2,1)} %get-tuple-element.4.errors, bf16[1,512,512]{2,1,0:T(8,128)(2,1)} %bitcast.7), custom_call_target="tpu_custom_call" | custom-call | tf_op jit(solution)/shard_map/pallas_call | solution.py:443

commit v3 on v2

--- a/solution.py
+++ b/solution.py
@@ -8,7 +8,7 @@
 MESH = pl.DeviceIdType.MESH
 BF16 = jnp.bfloat16
 F32 = jnp.float32
-DIRECT_Z = (3, 0)
+DIRECT_Z = (3, 2, 1, 0)
 DIRECT_X = (0,)
 
 
@@ -36,6 +36,7 @@
     xs, own, xr, zf, zs, zr, ps, pr, ef, eg, acc, gs, ga, gt, gb,
     load_sem, w_ss, w_rs, xa_ss, xa_rs, xb_ss, xb_rs, zf_ss, zf_rs, fc_ss, fc_rs, fy_ss, fy_rs, ff_ss, ff_rs,
     x_ss, x_rs, z_ss, z_rs, p_ss, p_rs, az_ss, az_rs, ax_ss, ax_rs, ay_ss, ay_rs, gc_ss, gc_rs, gy_ss, gy_rs,
+    hh, hy_ss, hy_rs, hc_ss, hc_rs, hf_ss, hf_rs,
 ):
     l, r, f = lax.axis_index("layer"), lax.axis_index("rows"), lax.axis_index("feat")
     yh, c = l // 2, l % 2
@@ -112,26 +113,32 @@
     def features(chunk):
         left, right = xg[0, chunk], xg[1, chunk]
         pre = dot(left, ew[:1152]) + dot(right, ew[1152:]) + enc_b[...]
-        fh[l, chunk, :, :512] = jnp.maximum(pre, 0.0).astype(BF16)
-        gate = dot_t(left, gw[:, :1152]) + dot_t(right, gw[:, 1152:])
-        up = dot_t(left, uw[:, :1152]) + dot_t(right, uw[:, 1152:])
-        fh[l, chunk, :, 512:] = (gelu(gate) * up).astype(BF16)
+        fh[l, chunk] = jnp.maximum(pre, 0.0).astype(BF16)
+        gate = dot_t(gw[:, :1152], left) + dot_t(gw[:, 1152:], right)
+        up = dot_t(uw[:, :1152], left) + dot_t(uw[:, 1152:], right)
+        hh[l, chunk] = (gelu(gate) * up).astype(BF16)
 
     def share(d):
         chunk = (r - d) % 4
         features(chunk)
         send(fh.at[l, chunk], fh.at[l, chunk], fy_ss.at[d], fy_rs.at[d], far_peer)
+        send(hh.at[l, chunk], hh.at[l, chunk], hy_ss.at[d], hy_rs.at[d], far_peer)
         send(fh.at[l, chunk], fh.at[l, chunk], fc_ss.at[d], fc_rs.at[d], core_peer)
+        send(hh.at[l, chunk], hh.at[l, chunk], hc_ss.at[d], hc_rs.at[d], core_peer)
 
     def hand_on(d):
         chunk = (r - d) % 4
         arrived(fh.at[far_l, chunk], fy_ss.at[d], fy_rs.at[d])
+        arrived(hh.at[far_l, chunk], hy_ss.at[d], hy_rs.at[d])
         send(fh.at[far_l, chunk], fh.at[far_l, chunk], ff_ss.at[d], ff_rs.at[d], core_peer)
+        send(hh.at[far_l, chunk], hh.at[far_l, chunk], hf_ss.at[d], hf_rs.at[d], core_peer)
 
     def have(d):
         chunk = (r - d) % 4
         arrived(fh.at[core_l, chunk], fc_ss.at[d], fc_rs.at[d])
+        arrived(hh.at[core_l, chunk], hc_ss.at[d], hc_rs.at[d])
         arrived(fh.at[cross_l, chunk], ff_ss.at[d], ff_rs.at[d])
+        arrived(hh.at[cross_l, chunk], hf_ss.at[d], hf_rs.at[d])
 
     low, high = pl.ds(0, 64), pl.ds(64, 64)
 
@@ -155,9 +162,11 @@
         arrived(xg.at[other, chunk, high], zf_ss.at[d - 1, 1], zf_rs.at[d - 1, 1])
 
     def partial_sum(t, chunk):
-        total = -dot(fh[t, chunk, :, 512:], wd[t])
+        total = -lax.dot_general(
+            hh[t, chunk], wd[t], (((0,), (0,)), ((), ())), preferred_element_type=F32
+        )
         for s in range(t + 1):
-            total = total + dot_t(fh[s, chunk, :, :512], dv[pair_index(s, t)])
+            total = total + dot_t(fh[s, chunk], dv[pair_index(s, t)])
         return total
 
     def decode(d, targets):
@@ -335,7 +344,6 @@
     sum_z(2)
     sum_pair(2)
     gather_z(3)
-    relay_z(2)
     sum_x(1)
     gather_z(2)
     sum_x(0)
@@ -343,7 +351,6 @@
     sum_pair(1)
     pass_on(3)
     sum_z(0)
-    relay_z(1)
     sum_pair(0)
     gather_z(1)
     pass_on(2)
@@ -403,7 +410,7 @@
         vmem((4, 144, 576), BF16),
         vmem((4, 144, 576), BF16),
         vmem((10, 576, 512), BF16),
-        vmem((4, 4, 128, 656), BF16),
+        vmem((4, 4, 128, 512), BF16),
         vmem((4, 3, 128, 576), BF16),
         vmem((4, 128, 576), F32),
         vmem((4, 3, 128, 576), BF16),
@@ -423,6 +430,7 @@
     ]
     for shape in ((3,), (3,), (2,), (3, 2), (4,), (4,), (4,), (4, 3), (4, 7), (4,), (4, 7), (4, 3), (4, 2), (4, 4), (4, 4)):
         scratch += [dma(shape), dma(shape)]
+    scratch += [vmem((4, 4, 144, 128), BF16)] + [dma((4,)) for _ in range(6)]
     errors, act_grad = pl.pallas_call(
         kernel,
         out_shape=(

time: 116 us -> 115 us (level)
  Pallas kernels: 116 us -> 114 us
    pallas_call x1, Pallas kernels: 114 us -> 112 us  [body(): pl.pallas_call(kernel, out_shape=(jax.ShapeDtypeStruct((4, 8, 576), BF16)...]
where the time goes in v3:
time: 115 us
  Pallas kernels  114 us (99%)
    pallas_call x1, Pallas kernels, body(): pl.pallas_call(kernel, out_shape=(jax.ShapeDtypeStruct((4, 8, 576), BF16)...  112 us

profile of v3, /device:TPU:6, one launch (start us, length us, event | category | flops | bytes accessed | tf_op | source)
XLA Modules:
  0.0 114.7 jit_solution(14253121223232091760)
XLA Ops:
  0.6 112.1 %shard_map.104 = (bf16[4,8,576]{2,1,0:T(8,128)(2,1)}, bf16[512,512]{1,0:T(8,128)(2,1)}) custom-call(bf16[128,2304]{1,0:T(8,128)(2,1)} %bitcast.13, f32[1,2304]{1,0:T(1,128)} %gain.1, bf16[144,2304]{1,0:T(8,128)(2,1)} %bitcast.10, bf16[144,2304]{1,0:T(8,128)(2,1)} %bitcast.11, bf16[144,2304]{1,0:T(8,128)(2,1)} %bitcast.12, bf16[2304,512]{1,0:T(8,128)(2,1)} %bitcast.9, ...), custom_call_target="tpu_custom_call" | custom-call | flops 8200000000 | bytes 12000000 | tf_op jit(solution)/shard_map/pallas_call | solution.py:434
  112.8 1.9 %shard_map.105 = (bf16[8,4,576]{2,1,0:T(4,128)(2,1)}, bf16[1,512,512]{2,1,0:T(8,128)(2,1)}) custom-call(bf16[4,8,576]{2,1,0:T(8,128)(2,1)} %get-tuple-element.4.errors, bf16[1,512,512]{2,1,0:T(8,128)(2,1)} %bitcast.7), custom_call_target="tpu_custom_call" | custom-call | tf_op jit(solution)/shard_map/pallas_call | solution.py:451

commit v4 on v3

--- a/solution.py
+++ b/solution.py
@@ -9,7 +9,7 @@
 BF16 = jnp.bfloat16
 F32 = jnp.float32
 DIRECT_Z = (3, 2, 1, 0)
-DIRECT_X = (0,)
+DIRECT_X = (1, 0)
 
 
 def pair_index(source, target, layers=4):
@@ -364,7 +364,6 @@
     step(3, 0)
     step(3, 1)
     step(3, 3)
-    pass_on(1)
     step(3, 2)
     step(2, 0)
     core_sum(3, 0)

time: 115 us -> 115 us (level)
  no operation moved by 1% of the time
where the time goes in v4:
time: 115 us
  Pallas kernels  114 us (99%)
    pallas_call x1, Pallas kernels, body(): pl.pallas_call(kernel, out_shape=(jax.ShapeDtypeStruct((4, 8, 576), BF16)...  112 us

profile of v4, /device:TPU:6, one launch (start us, length us, event | category | flops | bytes accessed | tf_op | source)
XLA Modules:
  0.0 115.0 jit_solution(4758953559145812017)
XLA Ops:
  0.6 112.5 %shard_map.104 = (bf16[4,8,576]{2,1,0:T(8,128)(2,1)}, bf16[512,512]{1,0:T(8,128)(2,1)}) custom-call(bf16[128,2304]{1,0:T(8,128)(2,1)} %bitcast.13, f32[1,2304]{1,0:T(1,128)} %gain.1, bf16[144,2304]{1,0:T(8,128)(2,1)} %bitcast.10, bf16[144,2304]{1,0:T(8,128)(2,1)} %bitcast.11, bf16[144,2304]{1,0:T(8,128)(2,1)} %bitcast.12, bf16[2304,512]{1,0:T(8,128)(2,1)} %bitcast.9, ...), custom_call_target="tpu_custom_call" | custom-call | flops 8200000000 | bytes 12000000 | tf_op jit(solution)/shard_map/pallas_call | solution.py:433
  113.1 1.9 %shard_map.105 = (bf16[8,4,576]{2,1,0:T(4,128)(2,1)}, bf16[1,512,512]{2,1,0:T(8,128)(2,1)}) custom-call(bf16[4,8,576]{2,1,0:T(8,128)(2,1)} %get-tuple-element.4.errors, bf16[1,512,512]{2,1,0:T(8,128)(2,1)} %bitcast.7), custom_call_target="tpu_custom_call" | custom-call | tf_op jit(solution)/shard_map/pallas_call | solution.py:450

commit v5 on v3

--- a/solution.py
+++ b/solution.py
@@ -307,6 +307,12 @@
         @pl.when((c == s % 2) & (yh != s // 2))
         def _():
             far_copy(s, d).wait_send()
+
+    order = (0, 1, 3, 2)
+
+    def step(t, d):
+        gradient(t, d)
+        core_send(t, d)
 
     share(0)
     relay(1)
@@ -346,27 +352,21 @@
     gather_z(3)
     sum_x(1)
     gather_z(2)
+    step(3, 0)
     sum_x(0)
     sum_z(1)
     sum_pair(1)
     pass_on(3)
     sum_z(0)
+    step(2, 0)
     sum_pair(0)
     gather_z(1)
     pass_on(2)
+    step(3, 1)
     gather_z(0)
-    order = (0, 1, 3, 2)
-
-    def step(t, d):
-        gradient(t, d)
-        core_send(t, d)
-
-    step(3, 0)
-    step(3, 1)
     step(3, 3)
     pass_on(1)
     step(3, 2)
-    step(2, 0)
     core_sum(3, 0)
     step(2, 1)
     core_sum(3, 1)

time: 115 us -> 114 us (level)
  no operation moved by 1% of the time
where the time goes in v5:
time: 114 us
  Pallas kernels  113 us (99%)
    pallas_call x1, Pallas kernels, body(): pl.pallas_call(kernel, out_shape=(jax.ShapeDtypeStruct((4, 8, 576), BF16)...  111 us

profile of v5, /device:TPU:6, one launch (start us, length us, event | category | flops | bytes accessed | tf_op | source)
XLA Modules:
  0.0 113.8 jit_solution(6767830834107300427)
XLA Ops:
  0.6 111.3 %shard_map.104 = (bf16[4,8,576]{2,1,0:T(8,128)(2,1)}, bf16[512,512]{1,0:T(8,128)(2,1)}) custom-call(bf16[128,2304]{1,0:T(8,128)(2,1)} %bitcast.13, f32[1,2304]{1,0:T(1,128)} %gain.1, bf16[144,2304]{1,0:T(8,128)(2,1)} %bitcast.10, bf16[144,2304]{1,0:T(8,128)(2,1)} %bitcast.11, bf16[144,2304]{1,0:T(8,128)(2,1)} %bitcast.12, bf16[2304,512]{1,0:T(8,128)(2,1)} %bitcast.9, ...), custom_call_target="tpu_custom_call" | custom-call | flops 8200000000 | bytes 12000000 | tf_op jit(solution)/shard_map/pallas_call | solution.py:434
  111.9 1.9 %shard_map.105 = (bf16[8,4,576]{2,1,0:T(4,128)(2,1)}, bf16[1,512,512]{2,1,0:T(8,128)(2,1)}) custom-call(bf16[4,8,576]{2,1,0:T(8,128)(2,1)} %get-tuple-element.4.errors, bf16[1,512,512]{2,1,0:T(8,128)(2,1)} %bitcast.7), custom_call_target="tpu_custom_call" | custom-call | tf_op jit(solution)/shard_map/pallas_call | solution.py:451
